TPU v7x, 32 devices: a whole 2x2x4 slice. The times are simulated.
32 devices in a mesh: ctx: 8 (over y, x, core), ch: 4 (over z).
Axes of the slice: x: 2, y: 2, z: 4, core: 2. Of those that a mesh axis runs over, the one named last changes fastest.
Arguments:
- projected: bfloat16 [3, 1536, 4096], P(None, 'ctx', 'ch'), may hold values from -6 to 6
- short_filter: float32 [7, 3, 4096], P(None, None, 'ch'), may hold values from -2.5 to 2.5
- medium_filter: bfloat16 [128, 4096], P(None, 'ch'), may hold values from -1.25 to 1.25
- decay: float32 [16, 4096], P(None, 'ch'), may hold values from 0.00013020834 to 0.05
- residues: float32 [16, 4096], P(None, 'ch'), may hold values from -3 to 3
- skip_gain: float32 [4096], P('ch'), may hold values from -6 to 6
- out_gain: float32 [4096], P('ch'), may hold values from 0.25 to 1.75
Outputs:
- mixed: bfloat16 [1536, 4096], P('ctx', 'ch')
All inputs are finite; a program needn't handle non-finite values.
Results may differ from a plain program's by a relative error of at most 0.014.
Values may be sent and summed in bfloat16 or wider, within the bound.
A program may use at most 128 MiB of HBM per device.

v0:
```python
import functools

import jax
import jax.numpy as jnp
from jax import lax
from jax.experimental import pallas as pl
from jax.experimental.pallas import tpu as pltpu
from jax.sharding import PartitionSpec as P

C = 4096
SHORT = 7
MED = 128
MODES = 16
LANES = 128
SUB = 8
LEAD = 8
TILE = 16
TAPS = 8
norm_eps = 1e-06
MESH = pl.DeviceIdType.MESH


def as_tokens(rows):
    return rows.reshape(rows.shape[0] // SUB, SUB, LANES)


def as_rows(tokens):
    return tokens.reshape(tokens.shape[0] * SUB, LANES)


def token_rows(first, count):
    start = first * SUB
    if not isinstance(start, int):
        start = pl.multiple_of(start, SUB)
    return pl.ds(start, count * SUB)


def rounded(tokens):
    return as_tokens(as_rows(tokens).astype(jnp.bfloat16).astype(jnp.float32))


def mode_sum(parts):
    count = parts.shape[0]
    while count > 1:
        count //= 2
        parts = parts[:count] + parts[count:]
    return parts[0]


def block_kernel(
    ctx_size,
    ch_size,
    proj_ref,
    short_ref,
    medium_ref,
    decay_ref,
    residue_ref,
    skip_ref,
    gain_ref,
    out_ref,
    series0,
    series1,
    series2,
    short_taps,
    medium_taps,
    product,
    queries,
    mediated,
    summed,
    rates,
    weights_buf,
    carry,
    squares,
    edge_recv,
    product_send,
    product_recv,
    state_send,
    state_recv,
    sum_send,
    sum_recv,
    edge_sems,
    product_sems,
    state_send_sems,
    state_recv_sems,
    sum_send_sems,
    sum_recv_sems,
):
    rows = proj_ref.shape[1]
    groups = proj_ref.shape[2] // LANES
    series = (series0, series1, series2)
    me = lax.axis_index("ctx")
    my_ch = lax.axis_index("ch")
    following = lax.rem(me + 1, ctx_size)

    barrier = pltpu.get_barrier_semaphore()
    for step in range(1, ctx_size):
        pl.semaphore_signal(
            barrier,
            inc=1,
            device_id={"ctx": lax.rem(me + step, ctx_size)},
            device_id_type=MESH,
        )
    for step in range(1, ch_size):
        pl.semaphore_signal(
            barrier,
            inc=1,
            device_id={"ch": lax.rem(my_ch + step, ch_size)},
            device_id_type=MESH,
        )

    if groups < SUB:
        for ref in (
            series0, series1, series2, short_taps, medium_taps, rates, weights_buf,
        ):
            ref[...] = jnp.zeros(ref.shape, ref.dtype)

    def lane_group(group):
        return slice(group * LANES, (group + 1) * LANES)

    def spread_series(index):
        @pl.loop(0, rows // TILE)
        def _(tile):
            first = pl.multiple_of(tile * TILE, TILE)
            for group in range(groups):
                part = proj_ref[index, pl.ds(first, TILE), lane_group(group)]
                series[index][
                    pl.ds((LEAD + first) * SUB + group, TILE, stride=SUB), :
                ] = part.astype(jnp.float32)

    for delay in range(SHORT):
        for group in range(groups):
            short_taps[pl.ds(delay * 3 * SUB + group, 3, stride=SUB), :] = short_ref[
                delay, :, lane_group(group)
            ]
    spread_series(1)
    spread_series(2)

    pl.semaphore_wait(barrier, ctx_size - 1 + ch_size - 1)

    edge_copy = pltpu.make_async_remote_copy(
        src_ref=proj_ref.at[:, pl.ds(rows - TILE, TILE), :],
        dst_ref=edge_recv,
        send_sem=edge_sems.at[0],
        recv_sem=edge_sems.at[1],
        device_id={"ctx": following},
        device_id_type=MESH,
    )
    product_copy = pltpu.make_async_remote_copy(
        src_ref=product_send,
        dst_ref=product_recv,
        send_sem=product_sems.at[0],
        recv_sem=product_sems.at[1],
        device_id={"ctx": following},
        device_id_type=MESH,
    )

    @pl.when(me < ctx_size - 1)
    def _():
        edge_copy.start()

    def featured(index, first):
        window = as_tokens(series[index][token_rows(LEAD + first - (SHORT - 1), TILE + SHORT - 1), :])
        total = None
        for delay in range(SHORT):
            tap = short_taps[(delay * 3 + index) * SUB : (delay * 3 + index + 1) * SUB, :]
            offset = SHORT - 1 - delay
            term = tap[None] * window[offset : offset + TILE]
            total = term if total is None else total + term
        return rounded(total)

    def product_tile(first):
        return as_rows(featured(1, first) * featured(2, first)).astype(jnp.bfloat16)

    own_first = rows - MED

    @pl.loop(own_first // TILE, rows // TILE)
    def _(tile):
        first = tile * TILE
        value = product_tile(first)
        product_send[
            pl.ds(pl.multiple_of((first - own_first) * SUB, TILE * SUB), TILE * SUB), :
        ] = value
        product[token_rows(MED + first, TILE), :] = value.astype(jnp.float32)

    @pl.when(me < ctx_size - 1)
    def _():
        product_copy.start()

    @pl.loop(0, MED // TILE)
    def _(tile):
        first = pl.multiple_of(tile * TILE, TILE)
        for group in range(groups):
            part = medium_ref[pl.ds(first, TILE), lane_group(group)]
            medium_taps[pl.ds(first * SUB + group, TILE, stride=SUB), :] = part.astype(jnp.float32)

    spread_series(0)

    for group in range(groups):
        rate = decay_ref[:, lane_group(group)]
        twice = 2.0 * rate
        series_form = twice * (
            1.0
            - twice
            * (0.5 - twice * (1.0 / 6.0 - twice * (1.0 / 24.0 - twice * (1.0 / 120.0 - twice / 720.0))))
        )
        power = jnp.where(twice < 0.125, series_form, 1.0 - jnp.exp(-twice))
        rates[pl.ds(group, MODES, stride=SUB), :] = rate
        weights_buf[pl.ds(group, MODES, stride=SUB), :] = residue_ref[
            :, lane_group(group)
        ] * jnp.sqrt(power)

    @pl.when(me > 0)
    def _():
        edge_copy.wait_recv()
        for index in range(3):
            for group in range(groups):
                part = edge_recv[index, :, lane_group(group)].astype(jnp.float32)
                series[index][pl.ds(group, LEAD, stride=SUB), :] = part[TILE - LEAD :]

    @pl.when(me == 0)
    def _():
        for index in range(3):
            series[index][0 : LEAD * SUB, :] = jnp.zeros((LEAD * SUB, LANES), jnp.float32)

    @pl.loop(0, own_first // TILE)
    def _(tile):
        first = tile * TILE
        product[token_rows(MED + first, TILE), :] = product_tile(first).astype(jnp.float32)

    @pl.loop(0, rows // TILE)
    def _(tile):
        first = tile * TILE
        queries[token_rows(first, TILE), :] = as_rows(featured(0, first))

    def medium_tile(tile):
        first = tile * TILE

        def add_taps(step, total):
            delay = step * TAPS
            window = as_tokens(
                product[token_rows(MED + first - delay - (TAPS - 1), TILE + TAPS - 1), :]
            )
            taps = as_tokens(medium_taps[token_rows(delay, TAPS), :])
            for within in range(TAPS):
                offset = TAPS - 1 - within
                total = total + taps[within][None] * window[offset : offset + TILE]
            return total

        total = lax.fori_loop(
            0, MED // TAPS, add_taps, jnp.zeros((TILE, SUB, LANES), jnp.float32)
        )
        mediated[token_rows(first, TILE), :] = as_rows(rounded(total))

    @pl.loop(MED // TILE, rows // TILE)
    def _(tile):
        medium_tile(tile)

    @pl.when(me > 0)
    def _():
        product_copy.wait_recv()

        @pl.loop(0, MED // TILE)
        def _(tile):
            start = pl.multiple_of(tile * TILE * SUB, TILE * SUB)
            part = product_recv[pl.ds(start, TILE * SUB), :]
            product[pl.ds(start, TILE * SUB), :] = part.astype(jnp.float32)

    @pl.when(me == 0)
    def _():
        product[0 : MED * SUB, :] = jnp.zeros((MED * SUB, LANES), jnp.float32)

    @pl.loop(0, MED // TILE)
    def _(tile):
        medium_tile(tile)

    decay_step = jnp.exp(-as_tokens(rates[...]))
    weights = as_tokens(weights_buf[...])

    def state_step(step, state):
        inputs = as_tokens(mediated[token_rows(step * SUB, SUB), :])
        for within in range(SUB):
            state = decay_step * state + inputs[within][None]
        return state

    zero_state = jnp.zeros((MODES, SUB, LANES), jnp.float32)
    final = lax.fori_loop(0, rows // SUB, state_step, zero_state)
    state_send[...] = as_rows(final).astype(jnp.bfloat16)

    def state_copy(step):
        return pltpu.make_async_remote_copy(
            src_ref=state_send,
            dst_ref=state_recv.at[step - 1],
            send_sem=state_send_sems.at[step - 1],
            recv_sem=state_recv_sems.at[step - 1],
            device_id={"ctx": lax.rem(me + step, ctx_size)},
            device_id_type=MESH,
        )

    for step in range(1, ctx_size):
        @pl.when(me + step < ctx_size)
        def _():
            state_copy(step).start()

    skip = skip_ref[...]
    if groups < SUB:
        skip = jnp.concatenate([skip, jnp.zeros((SUB - groups, LANES), jnp.float32)], 0)

    def local_step(step, state):
        inputs = as_tokens(mediated[token_rows(step * SUB, SUB), :])
        sums = []
        for within in range(SUB):
            state = decay_step * state + inputs[within][None]
            sums.append((mode_sum(weights * state) + skip * inputs[within])[None])
        summed[token_rows(step * SUB, SUB), :] = as_rows(jnp.concatenate(sums, 0))
        return state

    lax.fori_loop(0, rows // SUB, local_step, zero_state)

    carry[...] = jnp.zeros(carry.shape, jnp.float32)
    for step in reversed(range(1, ctx_size)):
        @pl.when(me >= step)
        def _():
            state_copy(step).wait_recv()
            span = jnp.exp(-float(rows) * rates[...])
            carry[...] = carry[...] * span + state_recv[step - 1].astype(jnp.float32)

    def carried_step(step, state):
        queried = as_tokens(queries[token_rows(step * SUB, SUB), :])
        local = as_tokens(summed[token_rows(step * SUB, SUB), :])
        gated = []
        for within in range(SUB):
            state = decay_step * state
            gated.append((queried[within] * (local[within] + mode_sum(state)))[None])
        summed[token_rows(step * SUB, SUB), :] = as_rows(jnp.concatenate(gated, 0))
        return state

    lax.fori_loop(0, rows // SUB, carried_step, weights * as_tokens(carry[...]))

    padded = squares.shape[0]
    if padded > rows:
        squares[rows:padded, :] = jnp.zeros((padded - rows, LANES), jnp.float32)

    @pl.loop(0, rows // SUB)
    def _(tile):
        first = pl.multiple_of(tile * SUB, SUB)
        total = None
        for group in range(groups):
            part = summed[pl.ds(first * SUB + group, SUB, stride=SUB), :]
            total = part * part if total is None else total + part * part
        squares[pl.ds(first, SUB), :] = total

    own_sum = lax.dot_general(
        jnp.ones((SUB, LANES), jnp.float32),
        squares[...],
        (((1,), (1,)), ((), ())),
        precision=lax.Precision.HIGHEST,
        preferred_element_type=jnp.float32,
    )
    sum_send[...] = own_sum

    def sum_copy(step):
        return pltpu.make_async_remote_copy(
            src_ref=sum_send,
            dst_ref=sum_recv.at[step - 1],
            send_sem=sum_send_sems.at[step - 1],
            recv_sem=sum_recv_sems.at[step - 1],
            device_id={"ch": lax.rem(my_ch + step, ch_size)},
            device_id_type=MESH,
        )

    for step in range(1, ch_size):
        sum_copy(step).start()
    total_sum = own_sum
    for step in range(1, ch_size):
        sum_copy(step).wait_recv()
        total_sum = total_sum + sum_recv[step - 1]
    inverse = lax.rsqrt(total_sum / C + norm_eps)
    same = lax.broadcasted_iota(jnp.int32, (padded, padded), 0) == lax.broadcasted_iota(
        jnp.int32, (padded, padded), 1
    )
    column = jnp.sum(
        jnp.where(same, jnp.broadcast_to(inverse[0:1], (padded, padded)), 0.0), 1, keepdims=True
    )
    squares[...] = jnp.broadcast_to(column, (padded, LANES))

    @pl.loop(0, rows // TILE)
    def _(tile):
        first = pl.multiple_of(tile * TILE, TILE)
        scale = squares[pl.ds(first, TILE), :]
        for group in range(groups):
            part = summed[pl.ds(first * SUB + group, TILE, stride=SUB), :]
            out_ref[pl.ds(first, TILE), lane_group(group)] = (
                part * scale * gain_ref[:, lane_group(group)]
            ).astype(jnp.bfloat16)

    @pl.when(me < ctx_size - 1)
    def _():
        edge_copy.wait_send()
        product_copy.wait_send()

    for step in range(1, ctx_size):
        @pl.when(me + step < ctx_size)
        def _():
            state_copy(step).wait_send()

    for step in range(1, ch_size):
        sum_copy(step).wait_send()


def on_device(
    ctx_size, ch_size, projected, short_filter, medium_filter, decay, residues, skip_gain, out_gain
):
    rows = projected.shape[1]
    chans = projected.shape[2]
    padded = -(-rows // LANES) * LANES
    f32 = jnp.float32
    bf16 = jnp.bfloat16

    def token_buffer(count, dtype=f32):
        return pltpu.VMEM((count * SUB, LANES), dtype)

    dma = pltpu.SemaphoreType.DMA
    vmem = pl.BlockSpec(memory_space=pltpu.VMEM)
    flops = rows * chans * (2 * MED + 6 * SHORT + 8 * MODES)
    return pl.pallas_call(
        functools.partial(block_kernel, ctx_size, ch_size),
        out_shape=jax.ShapeDtypeStruct((rows, chans), bf16),
        in_specs=[vmem] * 7,
        out_specs=vmem,
        scratch_shapes=[
            token_buffer(LEAD + rows),
            token_buffer(LEAD + rows),
            token_buffer(LEAD + rows),
            token_buffer(SHORT * 3),
            token_buffer(MED),
            token_buffer(MED + rows),
            token_buffer(rows),
            token_buffer(rows),
            token_buffer(rows),
            token_buffer(MODES),
            token_buffer(MODES),
            token_buffer(MODES),
            pltpu.VMEM((padded, LANES), f32),
            pltpu.VMEM((3, TILE, chans), bf16),
            token_buffer(MED, bf16),
            token_buffer(MED, bf16),
            token_buffer(MODES, bf16),
            pltpu.VMEM((ctx_size - 1, MODES * SUB, LANES), bf16),
            pltpu.VMEM((SUB, padded), f32),
            pltpu.VMEM((ch_size - 1, SUB, padded), f32),
            dma((2,)),
            dma((2,)),
            dma((ctx_size - 1,)),
            dma((ctx_size - 1,)),
            dma((ch_size - 1,)),
            dma((ch_size - 1,)),
        ],
        compiler_params=pltpu.CompilerParams(
            collective_id=0, has_side_effects=True, vmem_limit_bytes=40 * 1024 * 1024
        ),
        cost_estimate=pl.CostEstimate(
            flops=flops, bytes_accessed=rows * chans * 8, transcendentals=0
        ),
    )(
        projected,
        short_filter,
        medium_filter,
        decay,
        residues,
        skip_gain.reshape(chans // LANES, LANES),
        out_gain.reshape(1, chans),
    )


def solution(mesh):
    in_specs = (
        P(None, "ctx", "ch"),
        P(None, None, "ch"),
        P(None, "ch"),
        P(None, "ch"),
        P(None, "ch"),
        P("ch"),
        P("ch"),
    )
    out_specs = P("ctx", "ch")
    body = functools.partial(on_device, mesh.shape["ctx"], mesh.shape["ch"])
    return jax.shard_map(
        body, mesh=mesh, in_specs=in_specs, out_specs=out_specs, check_vma=False
    )
```

profile of v0, /device:TPU:4, one launch (start us, length us, event | category | flops | bytes accessed | tf_op | source)
XLA Modules:
  0.0 32.5 jit_solution(4119989997242191176)
XLA Ops:
  0.0 1.0 %copy.8.short_ref = f32[7,3,1024]{2,1,0:T(4,128)S(1)} copy(f32[7,3,1024]{2,0,1:T(8,128)} %param.8) | data formatting | bytes 172032 | tf_op args[1]
  1.0 0.0 copy-start
  1.0 1.3 %copy-done = bf16[3,192,1024]{2,1,0:T(8,128)(2,1)S(1)} copy-done((bf16[3,192,1024]{2,1,0:T(8,128)(2,1)S(1)}, bf16[3,192,1024]{2,1,0:T(8,128)(2,1)}, u32[]{:S(2)}) %copy-start) | copy-done | bytes 1179672
  2.2 0.0 copy-start.1
  2.2 0.9 %copy-done.1 = bf16[128,1024]{1,0:T(8,128)(2,1)S(1)} copy-done((bf16[128,1024]{1,0:T(8,128)(2,1)S(1)}, bf16[128,1024]{1,0:T(8,128)(2,1)}, u32[]{:S(2)}) %copy-start.1) | copy-done | bytes 262168
  3.2 0.0 copy-start.2
  3.2 0.8 %copy-done.2 = f32[16,1024]{1,0:T(8,128)S(1)} copy-done((f32[16,1024]{1,0:T(8,128)S(1)}, f32[16,1024]{1,0:T(8,128)}, u32[]{:S(2)}) %copy-start.2) | copy-done | bytes 65560
  4.0 0.0 copy-start.3
  4.0 0.8 %copy-done.3 = f32[16,1024]{1,0:T(8,128)S(1)} copy-done((f32[16,1024]{1,0:T(8,128)S(1)}, f32[16,1024]{1,0:T(8,128)}, u32[]{:S(2)}) %copy-start.3) | copy-done | bytes 65560
  4.9 0.0 copy-start.4
  4.9 0.7 %copy-done.4 = f32[1024]{0:T(1024)S(1)} copy-done((f32[1024]{0:T(1024)S(1)}, f32[1024]{0:T(1024)}, u32[]{:S(2)}) %copy-start.4) | copy-done | bytes 4120
  5.5 0.0 copy-start.5
  5.6 0.7 %copy-done.5 = f32[1024]{0:T(1024)S(1)} copy-done((f32[1024]{0:T(1024)S(1)}, f32[1024]{0:T(1024)}, u32[]{:S(2)}) %copy-start.5) | copy-done | bytes 4120
  6.2 25.5 %shard_map.73 = bf16[192,1024]{1,0:T(8,128)(2,1)S(1)} custom-call(bf16[3,192,1024]{2,1,0:T(8,128)(2,1)S(1)} %copy-done, f32[7,3,1024]{2,1,0:T(4,128)S(1)} %copy.8.short_ref, bf16[128,1024]{1,0:T(8,128)(2,1)S(1)} %copy-done.1, f32[16,1024]{1,0:T(8,128)S(1)} %copy-done.2, f32[16,1024]{1,0:T(8,128)S(1)} %copy-done.3, f32[8,128]{1,0:T(8,128)S(1)} %bitcast.2, ...), custom_call_target="tpu_custom_call" | custom-call | flops 83755008 | bytes 1572864 | tf_op jit(solution)/shard_map/pallas_call | solution.py:425
  31.8 0.7 %copy.10 = bf16[192,1024]{1,0:T(8,128)(2,1)} copy(bf16[192,1024]{1,0:T(8,128)(2,1)S(1)} %shard_map.73) | data formatting | bytes 786432
Async XLA Ops:
  1.0 1.3 %copy-start = (bf16[3,192,1024]{2,1,0:T(8,128)(2,1)S(1)}, bf16[3,192,1024]{2,1,0:T(8,128)(2,1)}, u32[]{:S(2)}) copy-start(bf16[3,192,1024]{2,1,0:T(8,128)(2,1)} %proj_ref.1) | copy-start | bytes 3538948
  2.2 0.9 %copy-start.1 = (bf16[128,1024]{1,0:T(8,128)(2,1)S(1)}, bf16[128,1024]{1,0:T(8,128)(2,1)}, u32[]{:S(2)}) copy-start(bf16[128,1024]{1,0:T(8,128)(2,1)} %medium_ref.1) | copy-start | bytes 786436
  3.2 0.8 %copy-start.2 = (f32[16,1024]{1,0:T(8,128)S(1)}, f32[16,1024]{1,0:T(8,128)}, u32[]{:S(2)}) copy-start(f32[16,1024]{1,0:T(8,128)} %decay_ref.1) | copy-start | bytes 196612
  4.0 0.8 %copy-start.3 = (f32[16,1024]{1,0:T(8,128)S(1)}, f32[16,1024]{1,0:T(8,128)}, u32[]{:S(2)}) copy-start(f32[16,1024]{1,0:T(8,128)} %residue_ref.1) | copy-start | bytes 196612
  4.9 0.7 %copy-start.4 = (f32[1024]{0:T(1024)S(1)}, f32[1024]{0:T(1024)}, u32[]{:S(2)}) copy-start(f32[1024]{0:T(1024)} %param.12) | copy-start | bytes 12292
  5.5 0.7 %copy-start.5 = (f32[1024]{0:T(1024)S(1)}, f32[1024]{0:T(1024)}, u32[]{:S(2)}) copy-start(f32[1024]{0:T(1024)} %param.13) | copy-start | bytes 12292
where the time goes:
time: 32.9 us; the launch traced here: 32.5 us
  Pallas kernels  25.5 us (78%)
  local copies, waits for them, and re-layouts  6.97 us (21%)
    pallas_call x1, Pallas kernels, on_device(): pl.pallas_call(functools.partial(block_kernel, ctx_size, ch_size), out_sh...  25.5 us
    unnamed x14, local copies, waits for them, and re-layouts  6.97 us

commit v1 on v0

--- a/solution.py
+++ b/solution.py
@@ -50,6 +50,14 @@
 def block_kernel(
     ctx_size,
     ch_size,
+    proj_hbm,
+    short_hbm,
+    medium_hbm,
+    decay_hbm,
+    residue_hbm,
+    skip_hbm,
+    gain_hbm,
+    out_ref,
     proj_ref,
     short_ref,
     medium_ref,
@@ -57,7 +65,7 @@
     residue_ref,
     skip_ref,
     gain_ref,
-    out_ref,
+    load_sems,
     series0,
     series1,
     series2,
@@ -92,6 +100,24 @@
     my_ch = lax.axis_index("ch")
     following = lax.rem(me + 1, ctx_size)
 
+    pairs = {
+        "short": (short_hbm, short_ref),
+        "key": (proj_hbm.at[1], proj_ref.at[1]),
+        "value": (proj_hbm.at[2], proj_ref.at[2]),
+        "medium": (medium_hbm, medium_ref),
+        "query": (proj_hbm.at[0], proj_ref.at[0]),
+        "decay": (decay_hbm, decay_ref),
+        "residue": (residue_hbm, residue_ref),
+        "skip": (skip_hbm, skip_ref),
+        "gain": (gain_hbm, gain_ref),
+    }
+    loads = {
+        name: pltpu.make_async_copy(source, target, load_sems.at[position])
+        for position, (name, (source, target)) in enumerate(pairs.items())
+    }
+    for load in loads.values():
+        load.start()
+
     barrier = pltpu.get_barrier_semaphore()
     for step in range(1, ctx_size):
         pl.semaphore_signal(
@@ -127,18 +153,21 @@
                     pl.ds((LEAD + first) * SUB + group, TILE, stride=SUB), :
                 ] = part.astype(jnp.float32)
 
-    for delay in range(SHORT):
+    loads["short"].wait()
+    for index in range(3):
         for group in range(groups):
-            short_taps[pl.ds(delay * 3 * SUB + group, 3, stride=SUB), :] = short_ref[
-                delay, :, lane_group(group)
+            short_taps[pl.ds(index * SHORT * SUB + group, SHORT, stride=SUB), :] = short_ref[
+                index, :, lane_group(group)
             ]
+    loads["key"].wait()
     spread_series(1)
+    loads["value"].wait()
     spread_series(2)
 
     pl.semaphore_wait(barrier, ctx_size - 1 + ch_size - 1)
 
     edge_copy = pltpu.make_async_remote_copy(
-        src_ref=proj_ref.at[:, pl.ds(rows - TILE, TILE), :],
+        src_ref=proj_hbm.at[:, pl.ds(rows - TILE, TILE), :],
         dst_ref=edge_recv,
         send_sem=edge_sems.at[0],
         recv_sem=edge_sems.at[1],
@@ -162,7 +191,7 @@
         window = as_tokens(series[index][token_rows(LEAD + first - (SHORT - 1), TILE + SHORT - 1), :])
         total = None
         for delay in range(SHORT):
-            tap = short_taps[(delay * 3 + index) * SUB : (delay * 3 + index + 1) * SUB, :]
+            tap = short_taps[(index * SHORT + delay) * SUB : (index * SHORT + delay + 1) * SUB, :]
             offset = SHORT - 1 - delay
             term = tap[None] * window[offset : offset + TILE]
             total = term if total is None else total + term
@@ -186,6 +215,8 @@
     def _():
         product_copy.start()
 
+    loads["medium"].wait()
+
     @pl.loop(0, MED // TILE)
     def _(tile):
         first = pl.multiple_of(tile * TILE, TILE)
@@ -193,8 +224,11 @@
             part = medium_ref[pl.ds(first, TILE), lane_group(group)]
             medium_taps[pl.ds(first * SUB + group, TILE, stride=SUB), :] = part.astype(jnp.float32)
 
+    loads["query"].wait()
     spread_series(0)
 
+    loads["decay"].wait()
+    loads["residue"].wait()
     for group in range(groups):
         rate = decay_ref[:, lane_group(group)]
         twice = 2.0 * rate
@@ -301,6 +335,8 @@
         def _():
             state_copy(step).start()
 
+    loads["skip"].wait()
+    loads["gain"].wait()
     skip = skip_ref[...]
     if groups < SUB:
         skip = jnp.concatenate([skip, jnp.zeros((SUB - groups, LANES), jnp.float32)], 0)
@@ -425,9 +461,17 @@
     return pl.pallas_call(
         functools.partial(block_kernel, ctx_size, ch_size),
         out_shape=jax.ShapeDtypeStruct((rows, chans), bf16),
-        in_specs=[vmem] * 7,
+        in_specs=[pl.BlockSpec(memory_space=pltpu.HBM)] * 7,
         out_specs=vmem,
         scratch_shapes=[
+            pltpu.VMEM(projected.shape, bf16),
+            pltpu.VMEM((3, SHORT, chans), f32),
+            pltpu.VMEM(medium_filter.shape, bf16),
+            pltpu.VMEM(decay.shape, f32),
+            pltpu.VMEM(residues.shape, f32),
+            pltpu.VMEM((chans // LANES, LANES), f32),
+            pltpu.VMEM((1, chans), f32),
+            dma((9,)),
             token_buffer(LEAD + rows),
             token_buffer(LEAD + rows),
             token_buffer(LEAD + rows),
@@ -456,14 +500,14 @@
             dma((ch_size - 1,)),
         ],
         compiler_params=pltpu.CompilerParams(
-            collective_id=0, has_side_effects=True, vmem_limit_bytes=40 * 1024 * 1024
+            collective_id=0, has_side_effects=True, vmem_limit_bytes=63 * 1024 * 1024
         ),
         cost_estimate=pl.CostEstimate(
             flops=flops, bytes_accessed=rows * chans * 8, transcendentals=0
         ),
     )(
         projected,
-        short_filter,
+        jnp.transpose(short_filter, (1, 0, 2)),
         medium_filter,
         decay,
         residues,

time: 32.9 us -> 28.5 us (0.87)
  local copies, waits for them, and re-layouts: 6.97 us -> 1.77 us
  Pallas kernels: 25.5 us -> 26.6 us
    unnamed x14 -> x1, local copies, waits for them, and re-layouts: 6.97 us -> 1.77 us
    pallas_call x1, Pallas kernels: 25.5 us -> 26.6 us  [on_device(): pl.pallas_call(functools.partial(block_kernel, ctx_size, ch_size), out_sh...]
where the time goes in v1:
time: 28.5 us; the launch traced here: 28.4 us
  Pallas kernels  26.6 us (93%)
  local copies, waits for them, and re-layouts  1.77 us (6%)
    pallas_call x1, Pallas kernels, on_device(): pl.pallas_call(functools.partial(block_kernel, ctx_size, ch_size), out_sh...  26.6 us
    unnamed x1, local copies, waits for them, and re-layouts  1.77 us

profile of v1, /device:TPU:4, one launch (start us, length us, event | category | flops | bytes accessed | tf_op | source)
XLA Modules:
  0.0 28.4 jit_solution(15372543033531846131)
XLA Ops:
  0.0 26.6 %shard_map.73 = bf16[192,1024]{1,0:T(8,128)(2,1)} custom-call(bf16[3,192,1024]{2,1,0:T(8,128)(2,1)} %proj_hbm.1, f32[3,7,1024]{2,1,0:T(8,128)} %bitcast.3, bf16[128,1024]{1,0:T(8,128)(2,1)} %medium_hbm.1, f32[16,1024]{1,0:T(8,128)} %decay_hbm.1, f32[16,1024]{1,0:T(8,128)} %residue_hbm.1, f32[8,128]{1,0:T(8,128)} %bitcast.4, f32[1,1024]{1,0:T(1,128)} %bitcast.5), custom_call_target="tpu_custom_call" | custom-call | flops 83755008 | bytes 1572864 | tf_op jit(solution)/shard_map/pallas_call | solution.py:461
  26.6 1.8 %copy.9 = bf16[192,1024]{1,0:T(8,128)(2,1)} copy(bf16[192,1024]{1,0:T(8,128)(2,1)} %shard_map.73) | data formatting | bytes 786432

commit v2 on v1

--- a/solution.py
+++ b/solution.py
@@ -15,7 +15,9 @@
 SUB = 8
 LEAD = 8
 TILE = 16
-TAPS = 8
+GROUP = 16
+PAIRS = 4
+PAD = 1
 norm_eps = 1e-06
 MESH = pl.DeviceIdType.MESH
 
@@ -33,6 +35,10 @@
     if not isinstance(start, int):
         start = pl.multiple_of(start, SUB)
     return pl.ds(start, count * SUB)
+
+
+def as_pairs(rows):
+    return rows.reshape(rows.shape[0] // (2 * SUB), 2 * SUB, LANES)
 
 
 def rounded(tokens):
@@ -71,6 +77,9 @@
     series2,
     short_taps,
     medium_taps,
+    pair_taps,
+    even_pairs,
+    odd_pairs,
     product,
     queries,
     mediated,
@@ -200,7 +209,12 @@
     def product_tile(first):
         return as_rows(featured(1, first) * featured(2, first)).astype(jnp.bfloat16)
 
+    def keep_product(tile, value):
+        product[token_rows(PAD + MED + tile * TILE, TILE), :] = value.astype(jnp.float32)
+        even_pairs[pl.ds(MED // 2 + tile * (TILE // 2), TILE // 2)] = as_pairs(value)
+
     own_first = rows - MED
+    product[0 : PAD * SUB, :] = jnp.zeros((PAD * SUB, LANES), jnp.float32)
 
     @pl.loop(own_first // TILE, rows // TILE)
     def _(tile):
@@ -209,7 +223,7 @@
         product_send[
             pl.ds(pl.multiple_of((first - own_first) * SUB, TILE * SUB), TILE * SUB), :
         ] = value
-        product[token_rows(MED + first, TILE), :] = value.astype(jnp.float32)
+        keep_product(tile, value)
 
     @pl.when(me < ctx_size - 1)
     def _():
@@ -223,6 +237,8 @@
         for group in range(groups):
             part = medium_ref[pl.ds(first, TILE), lane_group(group)]
             medium_taps[pl.ds(first * SUB + group, TILE, stride=SUB), :] = part.astype(jnp.float32)
+        taps = as_tokens(medium_taps[token_rows(first, TILE), :])
+        pair_taps[pl.ds(first, TILE)] = jnp.concatenate([taps, taps], 1).astype(jnp.bfloat16)
 
     loads["query"].wait()
     spread_series(0)
@@ -258,34 +274,42 @@
 
     @pl.loop(0, own_first // TILE)
     def _(tile):
-        first = tile * TILE
-        product[token_rows(MED + first, TILE), :] = product_tile(first).astype(jnp.float32)
+        keep_product(tile, product_tile(tile * TILE))
 
     @pl.loop(0, rows // TILE)
     def _(tile):
         first = tile * TILE
         queries[token_rows(first, TILE), :] = as_rows(featured(0, first))
 
+    def shift_tile(tile):
+        first = tile * TILE
+        part = product[token_rows(first, TILE), :]
+        odd_pairs[pl.ds(tile * (TILE // 2), TILE // 2)] = as_pairs(part.astype(jnp.bfloat16))
+
     def medium_tile(tile):
-        first = tile * TILE
-
-        def add_taps(step, total):
-            delay = step * TAPS
-            window = as_tokens(
-                product[token_rows(MED + first - delay - (TAPS - 1), TILE + TAPS - 1), :]
-            )
-            taps = as_tokens(medium_taps[token_rows(delay, TAPS), :])
-            for within in range(TAPS):
-                offset = TAPS - 1 - within
-                total = total + taps[within][None] * window[offset : offset + TILE]
-            return total
-
-        total = lax.fori_loop(
-            0, MED // TAPS, add_taps, jnp.zeros((TILE, SUB, LANES), jnp.float32)
-        )
-        mediated[token_rows(first, TILE), :] = as_rows(rounded(total))
-
-    @pl.loop(MED // TILE, rows // TILE)
+        first_pair = tile * PAIRS
+        total = None
+        for delay in range(0, MED, GROUP):
+            start = (MED - delay - GROUP) // 2 + 1 + first_pair
+            even = even_pairs[pl.ds(start, PAIRS + GROUP // 2 - 1)]
+            odd = odd_pairs[pl.ds(start, PAIRS + GROUP // 2 - 1)]
+            terms = []
+            for within in range(GROUP):
+                window = odd if within % 2 else even
+                offset = GROUP // 2 - 1 - within // 2
+                terms.append(pair_taps[delay + within][None] * window[offset : offset + PAIRS])
+            while len(terms) > 1:
+                terms = [left + right for left, right in zip(terms[::2], terms[1::2])]
+            part = terms[0].astype(jnp.float32)
+            total = part if total is None else total + part
+        value = total.astype(jnp.bfloat16).astype(jnp.float32)
+        mediated[token_rows(first_pair * 2, PAIRS * 2), :] = value.reshape(PAIRS * 2 * SUB, LANES)
+
+    @pl.loop(MED // TILE, (MED + rows) // TILE)
+    def _(tile):
+        shift_tile(tile)
+
+    @pl.loop(MED // (2 * PAIRS), rows // (2 * PAIRS))
     def _(tile):
         medium_tile(tile)
 
@@ -297,13 +321,19 @@
         def _(tile):
             start = pl.multiple_of(tile * TILE * SUB, TILE * SUB)
             part = product_recv[pl.ds(start, TILE * SUB), :]
-            product[pl.ds(start, TILE * SUB), :] = part.astype(jnp.float32)
+            product[token_rows(PAD + tile * TILE, TILE), :] = part.astype(jnp.float32)
+            even_pairs[pl.ds(tile * (TILE // 2), TILE // 2)] = as_pairs(part)
 
     @pl.when(me == 0)
     def _():
-        product[0 : MED * SUB, :] = jnp.zeros((MED * SUB, LANES), jnp.float32)
-
-    @pl.loop(0, MED // TILE)
+        product[PAD * SUB : (PAD + MED) * SUB, :] = jnp.zeros((MED * SUB, LANES), jnp.float32)
+        even_pairs[0 : MED // 2] = jnp.zeros((MED // 2, 2 * SUB, LANES), jnp.bfloat16)
+
+    @pl.loop(0, MED // TILE + 1)
+    def _(tile):
+        shift_tile(tile)
+
+    @pl.loop(0, MED // (2 * PAIRS))
     def _(tile):
         medium_tile(tile)
 
@@ -477,7 +507,10 @@
             token_buffer(LEAD + rows),
             token_buffer(SHORT * 3),
             token_buffer(MED),
-            token_buffer(MED + rows),
+            pltpu.VMEM((MED, 2 * SUB, LANES), bf16),
+            pltpu.VMEM(((MED + rows) // 2, 2 * SUB, LANES), bf16),
+            pltpu.VMEM(((MED + rows) // 2, 2 * SUB, LANES), bf16),
+            token_buffer(PAD + MED + rows),
             token_buffer(rows),
             token_buffer(rows),
             token_buffer(rows),

time: 28.5 us -> 31.9 us (1.12)
  Pallas kernels: 26.6 us -> 30 us
    pallas_call x1, Pallas kernels: 26.6 us -> 30 us  [on_device(): pl.pallas_call(functools.partial(block_kernel, ctx_size, ch_size), out_sh...]
where the time goes in v2:
time: 31.9 us; the launch traced here: 31.7 us
  Pallas kernels  30 us (94%)
  local copies, waits for them, and re-layouts  1.77 us (6%)
    pallas_call x1, Pallas kernels, on_device(): pl.pallas_call(functools.partial(block_kernel, ctx_size, ch_size), out_sh...  30 us
    unnamed x1, local copies, waits for them, and re-layouts  1.77 us

profile of v2, /device:TPU:4, one launch (start us, length us, event | category | flops | bytes accessed | tf_op | source)
XLA Modules:
  0.0 31.7 jit_solution(13754205482530011839)
XLA Ops:
  0.0 30.0 %shard_map.73 = bf16[192,1024]{1,0:T(8,128)(2,1)} custom-call(bf16[3,192,1024]{2,1,0:T(8,128)(2,1)} %proj_hbm.1, f32[3,7,1024]{2,1,0:T(8,128)} %bitcast.3, bf16[128,1024]{1,0:T(8,128)(2,1)} %medium_hbm.1, f32[16,1024]{1,0:T(8,128)} %decay_hbm.1, f32[16,1024]{1,0:T(8,128)} %residue_hbm.1, f32[8,128]{1,0:T(8,128)} %bitcast.4, f32[1,1024]{1,0:T(1,128)} %bitcast.5), custom_call_target="tpu_custom_call" | custom-call | flops 83755008 | bytes 1572864 | tf_op jit(solution)/shard_map/pallas_call | solution.py:491
  30.0 1.8 %copy.9 = bf16[192,1024]{1,0:T(8,128)(2,1)} copy(bf16[192,1024]{1,0:T(8,128)(2,1)} %shard_map.73) | data formatting | bytes 786432

commit v3 on v1

--- a/solution.py
+++ b/solution.py
@@ -16,6 +16,9 @@
 LEAD = 8
 TILE = 16
 TAPS = 8
+PHASES = 4
+SUBS = 9
+DEPTH = MED // PHASES
 norm_eps = 1e-06
 MESH = pl.DeviceIdType.MESH
 
@@ -33,6 +36,18 @@
     if not isinstance(start, int):
         start = pl.multiple_of(start, SUB)
     return pl.ds(start, count * SUB)
+
+
+def phase_parts(tokens):
+    quads = tokens.reshape(tokens.shape[0] // PHASES, PHASES, SUB, LANES)
+    part00, part10, part01, part11 = (quads[:, phase] for phase in range(PHASES))
+    low, high = part00 + part10, part01 + part11
+    parts = (
+        part00, part01, part00 + part01,
+        part10, part11, part10 + part11,
+        low, high, low + high,
+    )
+    return [as_rows(part) for part in parts]
 
 
 def rounded(tokens):
@@ -71,7 +86,9 @@
     series2,
     short_taps,
     medium_taps,
-    product,
+    phased,
+    phased_taps,
+    filtered,
     queries,
     mediated,
     summed,
@@ -200,6 +217,11 @@
     def product_tile(first):
         return as_rows(featured(1, first) * featured(2, first)).astype(jnp.bfloat16)
 
+    def keep_product(first, tokens):
+        start = pl.multiple_of(first * (SUB // PHASES), TILE * SUB // PHASES)
+        for sub, part in enumerate(phase_parts(tokens)):
+            phased[sub, pl.ds(start, TILE * SUB // PHASES), :] = part
+
     own_first = rows - MED
 
     @pl.loop(own_first // TILE, rows // TILE)
@@ -209,7 +231,7 @@
         product_send[
             pl.ds(pl.multiple_of((first - own_first) * SUB, TILE * SUB), TILE * SUB), :
         ] = value
-        product[token_rows(MED + first, TILE), :] = value.astype(jnp.float32)
+        keep_product(MED + first, as_tokens(value.astype(jnp.float32)))
 
     @pl.when(me < ctx_size - 1)
     def _():
@@ -223,6 +245,10 @@
         for group in range(groups):
             part = medium_ref[pl.ds(first, TILE), lane_group(group)]
             medium_taps[pl.ds(first * SUB + group, TILE, stride=SUB), :] = part.astype(jnp.float32)
+        start = pl.multiple_of(tile * (TILE * SUB // PHASES), TILE * SUB // PHASES)
+        taps = as_tokens(medium_taps[token_rows(first, TILE), :])
+        for sub, part in enumerate(phase_parts(taps)):
+            phased_taps[sub, pl.ds(start, TILE * SUB // PHASES), :] = part
 
     loads["query"].wait()
     spread_series(0)
@@ -259,33 +285,56 @@
     @pl.loop(0, own_first // TILE)
     def _(tile):
         first = tile * TILE
-        product[token_rows(MED + first, TILE), :] = product_tile(first).astype(jnp.float32)
+        keep_product(MED + first, as_tokens(product_tile(first).astype(jnp.float32)))
 
     @pl.loop(0, rows // TILE)
     def _(tile):
         first = tile * TILE
         queries[token_rows(first, TILE), :] = as_rows(featured(0, first))
 
-    def medium_tile(tile):
-        first = tile * TILE
-
-        def add_taps(step, total):
-            delay = step * TAPS
+    steps = rows // PHASES
+
+    def sub_filter(sub, first, count):
+        total = jnp.zeros((count, SUB, LANES), jnp.float32)
+        for delay in range(0, DEPTH, TAPS):
             window = as_tokens(
-                product[token_rows(MED + first - delay - (TAPS - 1), TILE + TAPS - 1), :]
+                phased[sub, token_rows(DEPTH + first - delay - (TAPS - 1), count + TAPS - 1), :]
             )
-            taps = as_tokens(medium_taps[token_rows(delay, TAPS), :])
+            taps = as_tokens(phased_taps[sub, token_rows(delay, TAPS), :])
             for within in range(TAPS):
                 offset = TAPS - 1 - within
-                total = total + taps[within][None] * window[offset : offset + TILE]
-            return total
-
-        total = lax.fori_loop(
-            0, MED // TAPS, add_taps, jnp.zeros((TILE, SUB, LANES), jnp.float32)
+                total = total + taps[within][None] * window[offset : offset + count]
+        filtered[sub, token_rows(1 + first, count), :] = as_rows(total)
+
+    def medium_tile(tile):
+        @pl.loop(0, SUBS)
+        def _(sub):
+            sub_filter(sub, tile * TILE, TILE)
+
+    def merge_tile(tile):
+        count = TILE // PHASES
+        first = tile * count
+        wide = [
+            as_tokens(filtered[sub, token_rows(first, count + 1), :]) for sub in range(SUBS)
+        ]
+
+        def half_rate(base):
+            low, high, both = wide[base : base + 3]
+            return low[1:] + high[:count], both - low - high
+
+        even0, even1 = half_rate(0)
+        odd0, odd1 = half_rate(3)
+        both0, both1 = half_rate(6)
+        outs = (
+            even0 + odd1[:count],
+            both0 - even0 - odd0,
+            even1[1:] + odd0,
+            (both1 - even1 - odd1)[1:],
         )
-        mediated[token_rows(first, TILE), :] = as_rows(rounded(total))
-
-    @pl.loop(MED // TILE, rows // TILE)
+        tokens = jnp.stack(outs, 1).reshape(TILE, SUB, LANES)
+        mediated[token_rows(tile * TILE, TILE), :] = as_rows(rounded(tokens))
+
+    @pl.loop(DEPTH // TILE, steps // TILE)
     def _(tile):
         medium_tile(tile)
 
@@ -297,15 +346,23 @@
         def _(tile):
             start = pl.multiple_of(tile * TILE * SUB, TILE * SUB)
             part = product_recv[pl.ds(start, TILE * SUB), :]
-            product[pl.ds(start, TILE * SUB), :] = part.astype(jnp.float32)
+            keep_product(tile * TILE, as_tokens(part.astype(jnp.float32)))
 
     @pl.when(me == 0)
     def _():
-        product[0 : MED * SUB, :] = jnp.zeros((MED * SUB, LANES), jnp.float32)
-
-    @pl.loop(0, MED // TILE)
+        phased[:, 0 : DEPTH * SUB, :] = jnp.zeros((SUBS, DEPTH * SUB, LANES), jnp.float32)
+
+    @pl.loop(0, DEPTH // TILE)
     def _(tile):
         medium_tile(tile)
+
+    @pl.loop(0, SUBS)
+    def _(sub):
+        sub_filter(sub, -1, 1)
+
+    @pl.loop(0, rows // TILE)
+    def _(tile):
+        merge_tile(tile)
 
     decay_step = jnp.exp(-as_tokens(rates[...]))
     weights = as_tokens(weights_buf[...])
@@ -477,7 +534,9 @@
             token_buffer(LEAD + rows),
             token_buffer(SHORT * 3),
             token_buffer(MED),
-            token_buffer(MED + rows),
+            pltpu.VMEM((SUBS, (DEPTH + rows // PHASES) * SUB, LANES), f32),
+            pltpu.VMEM((SUBS, DEPTH * SUB, LANES), f32),
+            pltpu.VMEM((SUBS, (1 + rows // PHASES) * SUB, LANES), f32),
             token_buffer(rows),
             token_buffer(rows),
             token_buffer(rows),

time: 28.5 us -> 26.1 us (0.916)
  Pallas kernels: 26.6 us -> 24.2 us
    pallas_call x1, Pallas kernels: 26.6 us -> 24.2 us  [on_device(): pl.pallas_call(functools.partial(block_kernel, ctx_size, ch_size), out_sh...]
where the time goes in v3:
time: 26.1 us; the launch traced here: 26 us
  Pallas kernels  24.2 us (93%)
  local copies, waits for them, and re-layouts  1.77 us (7%)
    pallas_call x1, Pallas kernels, on_device(): pl.pallas_call(functools.partial(block_kernel, ctx_size, ch_size), out_sh...  24.2 us
    unnamed x1, local copies, waits for them, and re-layouts  1.77 us

profile of v3, /device:TPU:4, one launch (start us, length us, event | category | flops | bytes accessed | tf_op | source)
XLA Modules:
  0.0 26.0 jit_solution(10335005341303049078)
XLA Ops:
  0.0 24.2 %shard_map.73 = bf16[192,1024]{1,0:T(8,128)(2,1)} custom-call(bf16[3,192,1024]{2,1,0:T(8,128)(2,1)} %proj_hbm.1, f32[3,7,1024]{2,1,0:T(8,128)} %bitcast.3, bf16[128,1024]{1,0:T(8,128)(2,1)} %medium_hbm.1, f32[16,1024]{1,0:T(8,128)} %decay_hbm.1, f32[16,1024]{1,0:T(8,128)} %residue_hbm.1, f32[8,128]{1,0:T(8,128)} %bitcast.4, f32[1,1024]{1,0:T(1,128)} %bitcast.5), custom_call_target="tpu_custom_call" | custom-call | flops 83755008 | bytes 1572864 | tf_op jit(solution)/shard_map/pallas_call | solution.py:518
  24.2 1.8 %copy.9 = bf16[192,1024]{1,0:T(8,128)(2,1)} copy(bf16[192,1024]{1,0:T(8,128)(2,1)} %shard_map.73) | data formatting | bytes 786432

commit v4 on v3

--- a/solution.py
+++ b/solution.py
@@ -160,8 +160,8 @@
     def lane_group(group):
         return slice(group * LANES, (group + 1) * LANES)
 
-    def spread_series(index):
-        @pl.loop(0, rows // TILE)
+    def spread_series(index, low, high):
+        @pl.loop(low, high)
         def _(tile):
             first = pl.multiple_of(tile * TILE, TILE)
             for group in range(groups):
@@ -176,13 +176,6 @@
             short_taps[pl.ds(index * SHORT * SUB + group, SHORT, stride=SUB), :] = short_ref[
                 index, :, lane_group(group)
             ]
-    loads["key"].wait()
-    spread_series(1)
-    loads["value"].wait()
-    spread_series(2)
-
-    pl.semaphore_wait(barrier, ctx_size - 1 + ch_size - 1)
-
     edge_copy = pltpu.make_async_remote_copy(
         src_ref=proj_hbm.at[:, pl.ds(rows - TILE, TILE), :],
         dst_ref=edge_recv,
@@ -191,18 +184,18 @@
         device_id={"ctx": following},
         device_id_type=MESH,
     )
-    product_copy = pltpu.make_async_remote_copy(
-        src_ref=product_send,
-        dst_ref=product_recv,
-        send_sem=product_sems.at[0],
-        recv_sem=product_sems.at[1],
-        device_id={"ctx": following},
-        device_id_type=MESH,
-    )
-
-    @pl.when(me < ctx_size - 1)
-    def _():
-        edge_copy.start()
+    half_tiles = MED // (2 * TILE)
+    all_tiles = rows // TILE
+
+    def product_copy(half):
+        return pltpu.make_async_remote_copy(
+            src_ref=product_send.at[half],
+            dst_ref=product_recv.at[half],
+            send_sem=product_sems.at[0, half],
+            recv_sem=product_sems.at[1, half],
+            device_id={"ctx": following},
+            device_id_type=MESH,
+        )
 
     def featured(index, first):
         window = as_tokens(series[index][token_rows(LEAD + first - (SHORT - 1), TILE + SHORT - 1), :])
@@ -222,21 +215,52 @@
         for sub, part in enumerate(phase_parts(tokens)):
             phased[sub, pl.ds(start, TILE * SUB // PHASES), :] = part
 
-    own_first = rows - MED
-
-    @pl.loop(own_first // TILE, rows // TILE)
-    def _(tile):
-        first = tile * TILE
-        value = product_tile(first)
-        product_send[
-            pl.ds(pl.multiple_of((first - own_first) * SUB, TILE * SUB), TILE * SUB), :
-        ] = value
-        keep_product(MED + first, as_tokens(value.astype(jnp.float32)))
+    def send_half(half):
+        low = all_tiles - half_tiles * (half + 1)
+
+        @pl.loop(low, low + half_tiles)
+        def _(tile):
+            first = tile * TILE
+            value = product_tile(first)
+            start = pl.multiple_of((tile - low) * (TILE * SUB), TILE * SUB)
+            product_send[half, pl.ds(start, TILE * SUB), :] = value
+            keep_product(MED + first, as_tokens(value.astype(jnp.float32)))
+
+    def receive_half(half):
+        @pl.when(me > 0)
+        def _():
+            product_copy(half).wait_recv()
+
+            @pl.loop(0, half_tiles)
+            def _(tile):
+                start = pl.multiple_of(tile * TILE * SUB, TILE * SUB)
+                part = product_recv[half, pl.ds(start, TILE * SUB), :].astype(jnp.float32)
+                keep_product((tile + half_tiles * (1 - half)) * TILE, as_tokens(part))
+
+    tail = all_tiles - half_tiles - 1
+    loads["key"].wait()
+    spread_series(1, tail, all_tiles)
+    loads["value"].wait()
+    spread_series(2, tail, all_tiles)
+    send_half(0)
+    pl.semaphore_wait(barrier, ctx_size - 1 + ch_size - 1)
 
     @pl.when(me < ctx_size - 1)
     def _():
-        product_copy.start()
-
+        edge_copy.start()
+        product_copy(0).start()
+
+    middle = tail - half_tiles
+    spread_series(1, middle, tail)
+    spread_series(2, middle, tail)
+    send_half(1)
+
+    @pl.when(me < ctx_size - 1)
+    def _():
+        product_copy(1).start()
+
+    spread_series(1, 0, middle)
+    spread_series(2, 0, middle)
     loads["medium"].wait()
 
     @pl.loop(0, MED // TILE)
@@ -251,7 +275,7 @@
             phased_taps[sub, pl.ds(start, TILE * SUB // PHASES), :] = part
 
     loads["query"].wait()
-    spread_series(0)
+    spread_series(0, 0, all_tiles)
 
     loads["decay"].wait()
     loads["residue"].wait()
@@ -282,7 +306,7 @@
         for index in range(3):
             series[index][0 : LEAD * SUB, :] = jnp.zeros((LEAD * SUB, LANES), jnp.float32)
 
-    @pl.loop(0, own_first // TILE)
+    @pl.loop(0, all_tiles - 2 * half_tiles)
     def _(tile):
         first = tile * TILE
         keep_product(MED + first, as_tokens(product_tile(first).astype(jnp.float32)))
@@ -334,27 +358,17 @@
         tokens = jnp.stack(outs, 1).reshape(TILE, SUB, LANES)
         mediated[token_rows(tile * TILE, TILE), :] = as_rows(rounded(tokens))
 
+    @pl.when(me == 0)
+    def _():
+        phased[:, 0 : DEPTH * SUB, :] = jnp.zeros((SUBS, DEPTH * SUB, LANES), jnp.float32)
+
     @pl.loop(DEPTH // TILE, steps // TILE)
     def _(tile):
         medium_tile(tile)
 
-    @pl.when(me > 0)
-    def _():
-        product_copy.wait_recv()
-
-        @pl.loop(0, MED // TILE)
-        def _(tile):
-            start = pl.multiple_of(tile * TILE * SUB, TILE * SUB)
-            part = product_recv[pl.ds(start, TILE * SUB), :]
-            keep_product(tile * TILE, as_tokens(part.astype(jnp.float32)))
-
-    @pl.when(me == 0)
-    def _():
-        phased[:, 0 : DEPTH * SUB, :] = jnp.zeros((SUBS, DEPTH * SUB, LANES), jnp.float32)
-
-    @pl.loop(0, DEPTH // TILE)
-    def _(tile):
-        medium_tile(tile)
+    for half in range(2):
+        receive_half(half)
+        medium_tile(1 - half)
 
     @pl.loop(0, SUBS)
     def _(sub):
@@ -489,7 +503,8 @@
     @pl.when(me < ctx_size - 1)
     def _():
         edge_copy.wait_send()
-        product_copy.wait_send()
+        for half in range(2):
+            product_copy(half).wait_send()
 
     for step in range(1, ctx_size):
         @pl.when(me + step < ctx_size)
@@ -517,7 +532,7 @@
     flops = rows * chans * (2 * MED + 6 * SHORT + 8 * MODES)
     return pl.pallas_call(
         functools.partial(block_kernel, ctx_size, ch_size),
-        out_shape=jax.ShapeDtypeStruct((rows, chans), bf16),
+        out_shape=pltpu.VMEM((rows, chans), bf16),
         in_specs=[pl.BlockSpec(memory_space=pltpu.HBM)] * 7,
         out_specs=vmem,
         scratch_shapes=[
@@ -545,33 +560,38 @@
             token_buffer(MODES),
             pltpu.VMEM((padded, LANES), f32),
             pltpu.VMEM((3, TILE, chans), bf16),
-            token_buffer(MED, bf16),
-            token_buffer(MED, bf16),
+            pltpu.VMEM((2, MED * SUB // 2, LANES), bf16),
+            pltpu.VMEM((2, MED * SUB // 2, LANES), bf16),
             token_buffer(MODES, bf16),
             pltpu.VMEM((ctx_size - 1, MODES * SUB, LANES), bf16),
             pltpu.VMEM((SUB, padded), f32),
             pltpu.VMEM((ch_size - 1, SUB, padded), f32),
             dma((2,)),
-            dma((2,)),
+            dma((2, 2)),
             dma((ctx_size - 1,)),
             dma((ctx_size - 1,)),
             dma((ch_size - 1,)),
             dma((ch_size - 1,)),
         ],
         compiler_params=pltpu.CompilerParams(
-            collective_id=0, has_side_effects=True, vmem_limit_bytes=63 * 1024 * 1024
+            collective_id=0, has_side_effects=True, vmem_limit_bytes=40 * 1024 * 1024
         ),
         cost_estimate=pl.CostEstimate(
             flops=flops, bytes_accessed=rows * chans * 8, transcendentals=0
         ),
     )(
-        projected,
-        jnp.transpose(short_filter, (1, 0, 2)),
-        medium_filter,
-        decay,
-        residues,
-        skip_gain.reshape(chans // LANES, LANES),
-        out_gain.reshape(1, chans),
+        *(
+            pltpu.with_memory_space_constraint(operand, pltpu.HBM)
+            for operand in (
+                projected,
+                jnp.transpose(short_filter, (1, 0, 2)),
+                medium_filter,
+                decay,
+                residues,
+                skip_gain.reshape(chans // LANES, LANES),
+                out_gain.reshape(1, chans),
+            )
+        )
     )
 
 

time: 26.1 us -> 23.9 us (0.916)
  Pallas kernels: 24.2 us -> 23 us
  local copies, waits for them, and re-layouts: 1.77 us -> 0.75 us
    pallas_call x1, Pallas kernels: 24.2 us -> 23 us  [on_device(): pl.pallas_call(functools.partial(block_kernel, ctx_size, ch_size), out_sh...]
    unnamed x1, local copies, waits for them, and re-layouts: 1.77 us -> 0.75 us
where the time goes in v4:
time: 23.9 us; the launch traced here: 23.7 us
  Pallas kernels  23 us (96%)
  local copies, waits for them, and re-layouts  0.75 us (3%)
    pallas_call x1, Pallas kernels, on_device(): pl.pallas_call(functools.partial(block_kernel, ctx_size, ch_size), out_sh...  23 us
    unnamed x1, local copies, waits for them, and re-layouts  0.75 us

profile of v4, /device:TPU:4, one launch (start us, length us, event | category | flops | bytes accessed | tf_op | source)
XLA Modules:
  0.0 23.7 jit_solution(7437066565132753390)
XLA Ops:
  0.0 23.0 %shard_map.73 = bf16[192,1024]{1,0:T(8,128)(2,1)S(1)} custom-call(bf16[3,192,1024]{2,1,0:T(8,128)(2,1)} %proj_hbm.1, f32[3,7,1024]{2,1,0:T(8,128)} %bitcast.3, bf16[128,1024]{1,0:T(8,128)(2,1)} %medium_hbm.1, f32[16,1024]{1,0:T(8,128)} %decay_hbm.1, f32[16,1024]{1,0:T(8,128)} %residue_hbm.1, f32[8,128]{1,0:T(8,128)} %bitcast.4, f32[1,1024]{1,0:T(1,128)} %bitcast.5), custom_call_target="tpu_custom_call" | custom-call | flops 83755008 | bytes 1572864 | tf_op jit(solution)/shard_map/pallas_call | solution.py:533
  23.0 0.7 %copy.9 = bf16[192,1024]{1,0:T(8,128)(2,1)} copy(bf16[192,1024]{1,0:T(8,128)(2,1)S(1)} %shard_map.73) | data formatting | bytes 786432

commit v5 on v4

--- a/solution.py
+++ b/solution.py
@@ -95,6 +95,10 @@
     rates,
     weights_buf,
     carry,
+    block_decay,
+    head_taps,
+    out_table,
+    entry_states,
     squares,
     edge_recv,
     product_send,
@@ -274,9 +278,6 @@
         for sub, part in enumerate(phase_parts(taps)):
             phased_taps[sub, pl.ds(start, TILE * SUB // PHASES), :] = part
 
-    loads["query"].wait()
-    spread_series(0, 0, all_tiles)
-
     loads["decay"].wait()
     loads["residue"].wait()
     for group in range(groups):
@@ -293,6 +294,25 @@
             :, lane_group(group)
         ] * jnp.sqrt(power)
 
+    loads["skip"].wait()
+    loads["gain"].wait()
+    skip = skip_ref[...]
+    if groups < SUB:
+        skip = jnp.concatenate([skip, jnp.zeros((SUB - groups, LANES), jnp.float32)], 0)
+
+    decay_step = jnp.exp(-as_tokens(rates[...]))
+    weights = as_tokens(weights_buf[...])
+    block_decay[...] = jnp.exp(-float(TILE) * rates[...])
+    head_taps[0:SUB, :] = mode_sum(weights) + skip
+
+    def table_step(step, table):
+        table = decay_step * table
+        out_table[step] = as_rows(table)
+        head_taps[token_rows(step + 1, 1), :] = mode_sum(table)
+        return table
+
+    lax.fori_loop(0, TILE, table_step, weights)
+
     @pl.when(me > 0)
     def _():
         edge_copy.wait_recv()
@@ -310,11 +330,6 @@
     def _(tile):
         first = tile * TILE
         keep_product(MED + first, as_tokens(product_tile(first).astype(jnp.float32)))
-
-    @pl.loop(0, rows // TILE)
-    def _(tile):
-        first = tile * TILE
-        queries[token_rows(first, TILE), :] = as_rows(featured(0, first))
 
     steps = rows // PHASES
 
@@ -378,17 +393,17 @@
     def _(tile):
         merge_tile(tile)
 
-    decay_step = jnp.exp(-as_tokens(rates[...]))
-    weights = as_tokens(weights_buf[...])
-
-    def state_step(step, state):
-        inputs = as_tokens(mediated[token_rows(step * SUB, SUB), :])
-        for within in range(SUB):
-            state = decay_step * state + inputs[within][None]
+    zero_state = jnp.zeros((MODES, SUB, LANES), jnp.float32)
+
+    def state_step(block, state):
+        entry_states[block] = as_rows(state)
+        inputs = as_tokens(mediated[token_rows(block * TILE, TILE), :])
+        step_decay = jnp.exp(-as_tokens(rates[...]))
+        for within in range(TILE):
+            state = step_decay * state + inputs[within][None]
         return state
 
-    zero_state = jnp.zeros((MODES, SUB, LANES), jnp.float32)
-    final = lax.fori_loop(0, rows // SUB, state_step, zero_state)
+    final = lax.fori_loop(0, all_tiles, state_step, zero_state)
     state_send[...] = as_rows(final).astype(jnp.bfloat16)
 
     def state_copy(step):
@@ -406,22 +421,23 @@
         def _():
             state_copy(step).start()
 
-    loads["skip"].wait()
-    loads["gain"].wait()
-    skip = skip_ref[...]
-    if groups < SUB:
-        skip = jnp.concatenate([skip, jnp.zeros((SUB - groups, LANES), jnp.float32)], 0)
-
-    def local_step(step, state):
-        inputs = as_tokens(mediated[token_rows(step * SUB, SUB), :])
-        sums = []
-        for within in range(SUB):
-            state = decay_step * state + inputs[within][None]
-            sums.append((mode_sum(weights * state) + skip * inputs[within])[None])
-        summed[token_rows(step * SUB, SUB), :] = as_rows(jnp.concatenate(sums, 0))
-        return state
-
-    lax.fori_loop(0, rows // SUB, local_step, zero_state)
+    loads["query"].wait()
+    spread_series(0, 0, all_tiles)
+
+    @pl.loop(0, rows // TILE)
+    def _(tile):
+        first = tile * TILE
+        queries[token_rows(first, TILE), :] = as_rows(featured(0, first))
+
+    @pl.loop(0, all_tiles)
+    def _(block):
+        inputs = as_tokens(mediated[token_rows(block * TILE, TILE), :])
+        taps = as_tokens(head_taps[0 : TILE * SUB, :])
+        sums = [taps[0] * inputs[step] for step in range(TILE)]
+        for delay in range(1, TILE):
+            for step in range(delay, TILE):
+                sums[step] = sums[step] + taps[delay] * inputs[step - delay]
+        summed[token_rows(block * TILE, TILE), :] = as_rows(jnp.stack(sums, 0))
 
     carry[...] = jnp.zeros(carry.shape, jnp.float32)
     for step in reversed(range(1, ctx_size)):
@@ -431,17 +447,22 @@
             span = jnp.exp(-float(rows) * rates[...])
             carry[...] = carry[...] * span + state_recv[step - 1].astype(jnp.float32)
 
-    def carried_step(step, state):
-        queried = as_tokens(queries[token_rows(step * SUB, SUB), :])
-        local = as_tokens(summed[token_rows(step * SUB, SUB), :])
-        gated = []
-        for within in range(SUB):
-            state = decay_step * state
-            gated.append((queried[within] * (local[within] + mode_sum(state)))[None])
-        summed[token_rows(step * SUB, SUB), :] = as_rows(jnp.concatenate(gated, 0))
-        return state
-
-    lax.fori_loop(0, rows // SUB, carried_step, weights * as_tokens(carry[...]))
+    @pl.loop(0, all_tiles // 2)
+    def _(pair):
+        states = []
+        for member in range(2):
+            arrived = carry[...]
+            states.append(as_tokens(entry_states[pair * 2 + member] + arrived))
+            carry[...] = arrived * block_decay[...]
+        sums = ([], [])
+        for step in range(TILE):
+            table = as_tokens(out_table[step])
+            for member in range(2):
+                sums[member].append(mode_sum(table * states[member]))
+        for member in range(2):
+            here = token_rows((pair * 2 + member) * TILE, TILE)
+            total = as_rows(jnp.stack(sums[member], 0)) + summed[here, :]
+            summed[here, :] = queries[here, :] * total
 
     padded = squares.shape[0]
     if padded > rows:
@@ -558,6 +579,10 @@
             token_buffer(MODES),
             token_buffer(MODES),
             token_buffer(MODES),
+            token_buffer(MODES),
+            token_buffer(TILE + 1),
+            pltpu.VMEM((TILE, MODES * SUB, LANES), f32),
+            pltpu.VMEM((rows // TILE, MODES * SUB, LANES), f32),
             pltpu.VMEM((padded, LANES), f32),
             pltpu.VMEM((3, TILE, chans), bf16),
             pltpu.VMEM((2, MED * SUB // 2, LANES), bf16),

time: 23.9 us -> 23.6 us (0.987)
  Pallas kernels: 23 us -> 22.7 us
    pallas_call x1, Pallas kernels: 23 us -> 22.7 us  [on_device(): pl.pallas_call(functools.partial(block_kernel, ctx_size, ch_size), out_sh...]
where the time goes in v5:
time: 23.6 us; the launch traced here: 23.4 us
  Pallas kernels  22.7 us (96%)
  local copies, waits for them, and re-layouts  0.75 us (3%)
    pallas_call x1, Pallas kernels, on_device(): pl.pallas_call(functools.partial(block_kernel, ctx_size, ch_size), out_sh...  22.7 us
    unnamed x1, local copies, waits for them, and re-layouts  0.75 us

profile of v5, /device:TPU:4, one launch (start us, length us, event | category | flops | bytes accessed | tf_op | source)
XLA Modules:
  0.0 23.4 jit_solution(12560892490992845022)
XLA Ops:
  0.0 22.7 %shard_map.73 = bf16[192,1024]{1,0:T(8,128)(2,1)S(1)} custom-call(bf16[3,192,1024]{2,1,0:T(8,128)(2,1)} %proj_hbm.1, f32[3,7,1024]{2,1,0:T(8,128)} %bitcast.3, bf16[128,1024]{1,0:T(8,128)(2,1)} %medium_hbm.1, f32[16,1024]{1,0:T(8,128)} %decay_hbm.1, f32[16,1024]{1,0:T(8,128)} %residue_hbm.1, f32[8,128]{1,0:T(8,128)} %bitcast.4, f32[1,1024]{1,0:T(1,128)} %bitcast.5), custom_call_target="tpu_custom_call" | custom-call | flops 83755008 | bytes 1572864 | tf_op jit(solution)/shard_map/pallas_call | solution.py:554
  22.7 0.7 %copy.9 = bf16[192,1024]{1,0:T(8,128)(2,1)} copy(bf16[192,1024]{1,0:T(8,128)(2,1)S(1)} %shard_map.73) | data formatting | bytes 786432

commit v6 on v5

--- a/solution.py
+++ b/solution.py
@@ -48,6 +48,12 @@
         low, high, low + high,
     )
     return [as_rows(part) for part in parts]
+
+
+def gather_groups(parts):
+    blank = jnp.zeros(parts[0].shape, jnp.float32)
+    parts = list(parts) + [blank] * (SUB - len(parts))
+    return jnp.transpose(jnp.stack(parts, 0), (1, 0, 2))
 
 
 def rounded(tokens):
@@ -85,7 +91,6 @@
     series1,
     series2,
     short_taps,
-    medium_taps,
     phased,
     phased_taps,
     filtered,
@@ -99,6 +104,7 @@
     head_taps,
     out_table,
     entry_states,
+    flat,
     squares,
     edge_recv,
     product_send,
@@ -157,7 +163,7 @@
 
     if groups < SUB:
         for ref in (
-            series0, series1, series2, short_taps, medium_taps, rates, weights_buf,
+            series0, series1, series2, short_taps, rates, weights_buf,
         ):
             ref[...] = jnp.zeros(ref.shape, ref.dtype)
 
@@ -168,11 +174,13 @@
         @pl.loop(low, high)
         def _(tile):
             first = pl.multiple_of(tile * TILE, TILE)
-            for group in range(groups):
-                part = proj_ref[index, pl.ds(first, TILE), lane_group(group)]
-                series[index][
-                    pl.ds((LEAD + first) * SUB + group, TILE, stride=SUB), :
-                ] = part.astype(jnp.float32)
+            tokens = gather_groups(
+                [
+                    proj_ref[index, pl.ds(first, TILE), lane_group(group)].astype(jnp.float32)
+                    for group in range(groups)
+                ]
+            )
+            series[index][token_rows(LEAD + first, TILE), :] = as_rows(tokens)
 
     loads["short"].wait()
     for index in range(3):
@@ -270,11 +278,13 @@
     @pl.loop(0, MED // TILE)
     def _(tile):
         first = pl.multiple_of(tile * TILE, TILE)
-        for group in range(groups):
-            part = medium_ref[pl.ds(first, TILE), lane_group(group)]
-            medium_taps[pl.ds(first * SUB + group, TILE, stride=SUB), :] = part.astype(jnp.float32)
+        taps = gather_groups(
+            [
+                medium_ref[pl.ds(first, TILE), lane_group(group)].astype(jnp.float32)
+                for group in range(groups)
+            ]
+        )
         start = pl.multiple_of(tile * (TILE * SUB // PHASES), TILE * SUB // PHASES)
-        taps = as_tokens(medium_taps[token_rows(first, TILE), :])
         for sub, part in enumerate(phase_parts(taps)):
             phased_taps[sub, pl.ds(start, TILE * SUB // PHASES), :] = part
 
@@ -468,14 +478,16 @@
     if padded > rows:
         squares[rows:padded, :] = jnp.zeros((padded - rows, LANES), jnp.float32)
 
-    @pl.loop(0, rows // SUB)
+    @pl.loop(0, all_tiles)
     def _(tile):
-        first = pl.multiple_of(tile * SUB, SUB)
+        first = pl.multiple_of(tile * TILE, TILE)
+        parts = jnp.transpose(as_tokens(summed[token_rows(first, TILE), :]), (1, 0, 2))
         total = None
         for group in range(groups):
-            part = summed[pl.ds(first * SUB + group, SUB, stride=SUB), :]
+            part = parts[group]
             total = part * part if total is None else total + part * part
-        squares[pl.ds(first, SUB), :] = total
+            flat[pl.ds(first, TILE), lane_group(group)] = part
+        squares[pl.ds(first, TILE), :] = total
 
     own_sum = lax.dot_general(
         jnp.ones((SUB, LANES), jnp.float32),
@@ -516,7 +528,7 @@
         first = pl.multiple_of(tile * TILE, TILE)
         scale = squares[pl.ds(first, TILE), :]
         for group in range(groups):
-            part = summed[pl.ds(first * SUB + group, TILE, stride=SUB), :]
+            part = flat[pl.ds(first, TILE), lane_group(group)]
             out_ref[pl.ds(first, TILE), lane_group(group)] = (
                 part * scale * gain_ref[:, lane_group(group)]
             ).astype(jnp.bfloat16)
@@ -569,7 +581,6 @@
             token_buffer(LEAD + rows),
             token_buffer(LEAD + rows),
             token_buffer(SHORT * 3),
-            token_buffer(MED),
             pltpu.VMEM((SUBS, (DEPTH + rows // PHASES) * SUB, LANES), f32),
             pltpu.VMEM((SUBS, DEPTH * SUB, LANES), f32),
             pltpu.VMEM((SUBS, (1 + rows // PHASES) * SUB, LANES), f32),
@@ -583,6 +594,7 @@
             token_buffer(TILE + 1),
             pltpu.VMEM((TILE, MODES * SUB, LANES), f32),
             pltpu.VMEM((rows // TILE, MODES * SUB, LANES), f32),
+            pltpu.VMEM((rows, chans), f32),
             pltpu.VMEM((padded, LANES), f32),
             pltpu.VMEM((3, TILE, chans), bf16),
             pltpu.VMEM((2, MED * SUB // 2, LANES), bf16),

time: 23.6 us -> 23.5 us (level)
  no operation moved by 1% of the time
where the time goes in v6:
time: 23.5 us; the launch traced here: 23.3 us
  Pallas kernels  22.5 us (96%)
  local copies, waits for them, and re-layouts  0.75 us (3%)
    pallas_call x1, Pallas kernels, on_device(): pl.pallas_call(functools.partial(block_kernel, ctx_size, ch_size), out_sh...  22.5 us
    unnamed x1, local copies, waits for them, and re-layouts  0.75 us

profile of v6, /device:TPU:4, one launch (start us, length us, event | category | flops | bytes accessed | tf_op | source)
XLA Modules:
  0.0 23.3 jit_solution(13628797025100966614)
XLA Ops:
  0.0 22.5 %shard_map.73 = bf16[192,1024]{1,0:T(8,128)(2,1)S(1)} custom-call(bf16[3,192,1024]{2,1,0:T(8,128)(2,1)} %proj_hbm.1, f32[3,7,1024]{2,1,0:T(8,128)} %bitcast.3, bf16[128,1024]{1,0:T(8,128)(2,1)} %medium_hbm.1, f32[16,1024]{1,0:T(8,128)} %decay_hbm.1, f32[16,1024]{1,0:T(8,128)} %residue_hbm.1, f32[8,128]{1,0:T(8,128)} %bitcast.4, f32[1,1024]{1,0:T(1,128)} %bitcast.5), custom_call_target="tpu_custom_call" | custom-call | flops 83755008 | bytes 1572864 | tf_op jit(solution)/shard_map/pallas_call | solution.py:566
  22.5 0.7 %copy.9 = bf16[192,1024]{1,0:T(8,128)(2,1)} copy(bf16[192,1024]{1,0:T(8,128)(2,1)S(1)} %shard_map.73) | data formatting | bytes 786432

commit v7 on v6

--- a/solution.py
+++ b/solution.py
@@ -304,25 +304,6 @@
             :, lane_group(group)
         ] * jnp.sqrt(power)
 
-    loads["skip"].wait()
-    loads["gain"].wait()
-    skip = skip_ref[...]
-    if groups < SUB:
-        skip = jnp.concatenate([skip, jnp.zeros((SUB - groups, LANES), jnp.float32)], 0)
-
-    decay_step = jnp.exp(-as_tokens(rates[...]))
-    weights = as_tokens(weights_buf[...])
-    block_decay[...] = jnp.exp(-float(TILE) * rates[...])
-    head_taps[0:SUB, :] = mode_sum(weights) + skip
-
-    def table_step(step, table):
-        table = decay_step * table
-        out_table[step] = as_rows(table)
-        head_taps[token_rows(step + 1, 1), :] = mode_sum(table)
-        return table
-
-    lax.fori_loop(0, TILE, table_step, weights)
-
     @pl.when(me > 0)
     def _():
         edge_copy.wait_recv()
@@ -426,10 +407,29 @@
             device_id_type=MESH,
         )
 
-    for step in range(1, ctx_size):
+    for step in reversed(range(1, ctx_size)):
         @pl.when(me + step < ctx_size)
         def _():
             state_copy(step).start()
+
+    loads["skip"].wait()
+    loads["gain"].wait()
+    skip = skip_ref[...]
+    if groups < SUB:
+        skip = jnp.concatenate([skip, jnp.zeros((SUB - groups, LANES), jnp.float32)], 0)
+
+    decay_step = jnp.exp(-as_tokens(rates[...]))
+    weights = as_tokens(weights_buf[...])
+    block_decay[...] = jnp.exp(-float(TILE) * rates[...])
+    head_taps[0:SUB, :] = mode_sum(weights) + skip
+
+    def table_step(step, table):
+        table = decay_step * table
+        out_table[step] = as_rows(table)
+        head_taps[token_rows(step + 1, 1), :] = mode_sum(table)
+        return table
+
+    lax.fori_loop(0, TILE, table_step, weights)
 
     loads["query"].wait()
     spread_series(0, 0, all_tiles)

time: 23.5 us -> 23.8 us (1.013)
  Pallas kernels: 22.5 us -> 22.9 us
    pallas_call x1, Pallas kernels: 22.5 us -> 22.9 us  [on_device(): pl.pallas_call(functools.partial(block_kernel, ctx_size, ch_size), out_sh...]
where the time goes in v7:
time: 23.8 us; the launch traced here: 23.6 us
  Pallas kernels  22.9 us (96%)
  local copies, waits for them, and re-layouts  0.75 us (3%)
    pallas_call x1, Pallas kernels, on_device(): pl.pallas_call(functools.partial(block_kernel, ctx_size, ch_size), out_sh...  22.9 us
    unnamed x1, local copies, waits for them, and re-layouts  0.75 us

profile of v7, /device:TPU:4, one launch (start us, length us, event | category | flops | bytes accessed | tf_op | source)
XLA Modules:
  0.0 23.6 jit_solution(612085223024089015)
XLA Ops:
  0.0 22.9 %shard_map.73 = bf16[192,1024]{1,0:T(8,128)(2,1)S(1)} custom-call(bf16[3,192,1024]{2,1,0:T(8,128)(2,1)} %proj_hbm.1, f32[3,7,1024]{2,1,0:T(8,128)} %bitcast.3, bf16[128,1024]{1,0:T(8,128)(2,1)} %medium_hbm.1, f32[16,1024]{1,0:T(8,128)} %decay_hbm.1, f32[16,1024]{1,0:T(8,128)} %residue_hbm.1, f32[8,128]{1,0:T(8,128)} %bitcast.4, f32[1,1024]{1,0:T(1,128)} %bitcast.5), custom_call_target="tpu_custom_call" | custom-call | flops 83755008 | bytes 1572864 | tf_op jit(solution)/shard_map/pallas_call | solution.py:566
  22.9 0.7 %copy.9 = bf16[192,1024]{1,0:T(8,128)(2,1)} copy(bf16[192,1024]{1,0:T(8,128)(2,1)S(1)} %shard_map.73) | data formatting | bytes 786432

commit v8 on v7

--- a/solution.py
+++ b/solution.py
@@ -407,7 +407,7 @@
             device_id_type=MESH,
         )
 
-    for step in reversed(range(1, ctx_size)):
+    for step in range(1, ctx_size):
         @pl.when(me + step < ctx_size)
         def _():
             state_copy(step).start()

time: 23.8 us -> 23.4 us (0.983)
  Pallas kernels: 22.9 us -> 22.5 us
    pallas_call x1, Pallas kernels: 22.9 us -> 22.5 us  [on_device(): pl.pallas_call(functools.partial(block_kernel, ctx_size, ch_size), out_sh...]
where the time goes in v8:
time: 23.4 us; the launch traced here: 23.3 us
  Pallas kernels  22.5 us (96%)
  local copies, waits for them, and re-layouts  0.75 us (3%)
    pallas_call x1, Pallas kernels, on_device(): pl.pallas_call(functools.partial(block_kernel, ctx_size, ch_size), out_sh...  22.5 us
    unnamed x1, local copies, waits for them, and re-layouts  0.75 us

profile of v8, /device:TPU:4, one launch (start us, length us, event | category | flops | bytes accessed | tf_op | source)
XLA Modules:
  0.0 23.3 jit_solution(11471527231927099528)
XLA Ops:
  0.0 22.5 %shard_map.73 = bf16[192,1024]{1,0:T(8,128)(2,1)S(1)} custom-call(bf16[3,192,1024]{2,1,0:T(8,128)(2,1)} %proj_hbm.1, f32[3,7,1024]{2,1,0:T(8,128)} %bitcast.3, bf16[128,1024]{1,0:T(8,128)(2,1)} %medium_hbm.1, f32[16,1024]{1,0:T(8,128)} %decay_hbm.1, f32[16,1024]{1,0:T(8,128)} %residue_hbm.1, f32[8,128]{1,0:T(8,128)} %bitcast.4, f32[1,1024]{1,0:T(1,128)} %bitcast.5), custom_call_target="tpu_custom_call" | custom-call | flops 83755008 | bytes 1572864 | tf_op jit(solution)/shard_map/pallas_call | solution.py:566
  22.5 0.7 %copy.9 = bf16[192,1024]{1,0:T(8,128)(2,1)} copy(bf16[192,1024]{1,0:T(8,128)(2,1)S(1)} %shard_map.73) | data formatting | bytes 786432
